TPU v7x, 32 devices: a whole 2x2x4 slice. The times are simulated.
32 devices in a mesh: dp: 8 (over z, x), tensor: 4 (over y, core).
Axes of the slice: x: 2, y: 2, z: 4, core: 2. Of those that a mesh axis runs over, the one named last changes fastest.
Arguments:
- gate_grads: bfloat16 [8, 256, 8192], P('dp', 'tensor'), may hold values from -6 to 6
- up_grads: bfloat16 [8, 256, 8192], P('dp', 'tensor'), may hold values from -6 to 6
- gate_errors: bfloat16 [8, 256, 8192], P('dp', 'tensor'), may hold values from -3 to 3
- up_errors: bfloat16 [8, 256, 8192], P('dp', 'tensor'), may hold values from -3 to 3
- gate_start: float32 [8192, 32], replicated, may hold values from -6 to 6
- up_start: float32 [8192, 32], replicated, may hold values from -6 to 6
Outputs:
- gate_mean: bfloat16 [256, 8192], P('tensor')
- up_mean: bfloat16 [256, 8192], P('tensor')
- gate_new_errors: bfloat16 [8, 256, 8192], P('dp', 'tensor')
- up_new_errors: bfloat16 [8, 256, 8192], P('dp', 'tensor')
All inputs are finite; a program needn't handle non-finite values.
Results may differ from a plain program's by a relative error of at most 0.0015.
Values sent between devices are 32-bit elements; how exact they have to be, the bound alone decides.
A program may use at most 64 MiB of HBM per device.

v0:
```python
import jax
import jax.numpy as jnp
from jax import lax
from jax.sharding import PartitionSpec as P


def orthonormal(left, gram):
    lower = jnp.linalg.cholesky(gram)
    return lax.linalg.triangular_solve(lower, left, left_side=False, lower=True, transpose_a=True)


def inner(first, second):
    return jnp.dot(first.T, second, precision=lax.Precision.HIGHEST)


def per_device(gate_grads, up_grads, gate_errors, up_errors, gate_start, up_start):
    replicas = lax.axis_size("dp")
    gate_full = gate_grads[0].astype(jnp.float32) + gate_errors[0].astype(jnp.float32)
    up_full = up_grads[0].astype(jnp.float32) + up_errors[0].astype(jnp.float32)
    gate_term = jnp.dot(gate_full, gate_start, precision=lax.Precision.HIGHEST)
    up_term = jnp.dot(up_full, up_start, precision=lax.Precision.HIGHEST)
    gate_left, up_left = lax.psum((gate_term, up_term), "dp")
    gate_left = gate_left / replicas
    up_left = up_left / replicas
    gate_gram, up_gram = lax.psum((inner(gate_left, gate_left), inner(up_left, up_left)), "tensor")
    gate_basis = orthonormal(gate_left, gate_gram)
    up_basis = orthonormal(up_left, up_gram)
    gate_right, up_right = lax.psum(
        (inner(gate_full, gate_basis), inner(up_full, up_basis)), ("dp", "tensor")
    )
    gate_right = gate_right / replicas
    up_right = up_right / replicas
    gate_approx = jnp.dot(gate_basis, gate_right.T, precision=lax.Precision.HIGHEST)
    up_approx = jnp.dot(up_basis, up_right.T, precision=lax.Precision.HIGHEST)
    gate_new = (gate_full - gate_approx).astype(jnp.bfloat16)[None]
    up_new = (up_full - up_approx).astype(jnp.bfloat16)[None]
    return (gate_approx.astype(jnp.bfloat16), up_approx.astype(jnp.bfloat16), gate_new, up_new)


def solution(mesh):
    in_specs = (
        P("dp", "tensor", None),
        P("dp", "tensor", None),
        P("dp", "tensor", None),
        P("dp", "tensor", None),
        P(),
        P(),
    )
    out_specs = (
        P("tensor", None),
        P("tensor", None),
        P("dp", "tensor", None),
        P("dp", "tensor", None),
    )
    return jax.shard_map(
        per_device, mesh=mesh, in_specs=in_specs, out_specs=out_specs, check_vma=False
    )
```

profile of v0, /device:TPU:0, one launch (start us, length us, event | category | flops | bytes accessed | tf_op | source)
XLA Modules:
  0.0 229.0 jit_solution(3288730595172913577)
XLA Ops:
  7.2 0.0 copy-start
  7.2 0.0 all-reduce.5.cloned.1.call-start
  7.2 1.2 copy-done
  8.4 0.0 copy-start.3
  8.4 0.0 copy-start.6
  8.4 0.0 copy-start.9
  8.4 3.6 %fusion.7 = f32[64,32]{0,1:T(8,128)S(1)} fusion(f32[8192,32]{0,1:T(8,128)S(1)} %copy-done, bf16[1,64,8192]{2,1,0:T(8,128)(2,1)} %param.11, bf16[1,64,8192]{2,1,0:T(8,128)(2,1)} %param.9), kind=kOutput, calls=%fused_computation.9 | convolution fusion | flops 202899456 | bytes 3153920 | tf_op jit(solution)/shard_map/dot_general | solution.py:20
  12.0 0.0 copy-done.3
  12.0 0.0 copy-done.6
  12.0 0.0 copy-done.9
  12.0 0.0 copy-start.1
  12.0 0.0 copy-start.2
  12.0 1.9 fusion.2
  14.0 38.8 %all-reduce.1 = (f32[64,32]{0,1:T(8,128)S(1)}, f32[64,32]{0,1:T(8,128)S(1)}) all-reduce(f32[64,32]{0,1:T(8,128)S(1)} %fusion.7, f32[64,32]{0,1:T(8,128)S(1)} %fusion.2), channel_id=1, replica_groups=mesh['dp'=8,'tensor'=4] {'dp'}, use_global_device_ids=true, to_apply=%region_0.0 | all-reduce | flops 4096 | bytes 32768 | tf_op jit(solution)/shard_map/psum | solution.py:22
  52.8 0.1 fusion.28
  52.9 0.1 fusion.25
  53.1 10.5 %all-reduce.2 = (f32[32,32]{0,1:T(8,128)S(1)}, f32[32,32]{0,1:T(8,128)S(1)}) all-reduce(f32[32,32]{0,1:T(8,128)S(1)} %fusion.28, f32[32,32]{0,1:T(8,128)S(1)} %fusion.25), channel_id=1, replica_groups=mesh['dp'=8,'tensor'=4] {'tensor'}, use_global_device_ids=true, to_apply=%region_1.0 | all-reduce | flops 2048 | bytes 16384 | tf_op jit(solution)/shard_map/psum | solution.py:25
  63.6 0.1 copy.15
  63.6 0.1 copy.17
  63.7 2.9 %cholesky.55 = f32[32,32]{1,0:T(8,128)S(1)} custom-call(f32[32,32]{1,0:T(8,128)S(1)} %get-tuple-element.16), custom_call_target="Cholesky" | custom-call | tf_op jit(solution)/shard_map/jit(cholesky)/cholesky | solution.py:8
  66.7 0.6 compare_reduce_fusion
  67.3 0.7 fusion.19
  68.0 2.4 %custom-call.7 = f32[1,32,32]{1,2,0:T(8,128)S(1)} custom-call(f32[1,32,32]{2,1,0:T(8,128)S(1)} %fusion.19), custom_call_target="InvertDiagBlocksLowerTriangular" | custom-call | tf_op jit(solution)/shard_map/triangular_solve/custom-call.0 | solution.py:9
  70.4 0.2 convolution_bitcast_fusion
  70.7 2.9 %cholesky.44 = f32[32,32]{1,0:T(8,128)S(1)} custom-call(f32[32,32]{1,0:T(8,128)S(1)} %get-tuple-element.17), custom_call_target="Cholesky" | custom-call | tf_op jit(solution)/shard_map/jit(cholesky)/cholesky | solution.py:8
  73.6 0.6 compare_reduce_fusion.1
  74.3 0.7 fusion.18
  74.9 2.4 %custom-call.6 = f32[1,32,32]{1,2,0:T(8,128)S(1)} custom-call(f32[1,32,32]{2,1,0:T(8,128)S(1)} %fusion.18), custom_call_target="InvertDiagBlocksLowerTriangular" | custom-call | tf_op jit(solution)/shard_map/triangular_solve/custom-call.0 | solution.py:9
  77.4 0.2 convolution_bitcast_fusion.1
  77.6 0.0 copy-done.1
  77.6 0.0 copy-done.2
  77.6 0.0 copy-start.4
  77.6 0.0 copy-start.7
  77.6 2.5 %fusion.5 = f32[8192,32]{0,1:T(8,128)} fusion(f32[64,32]{0,1:T(8,128)S(1)} %convolution_bitcast_fusion.1, bf16[1,64,8192]{2,1,0:T(8,128)(2,1)S(1)} %copy-done.1, bf16[1,64,8192]{2,1,0:T(8,128)(2,1)S(1)} %copy-done.2), kind=kOutput, calls=%fused_computation.7 | convolution fusion | flops 202899456 | bytes 3153920 | tf_op jit(solution)/shard_map/dot_general | solution.py:13
  80.1 0.0 copy-done.4
  80.1 0.0 copy-done.7
  80.1 2.5 %fusion = f32[8192,32]{0,1:T(8,128)} fusion(f32[64,32]{0,1:T(8,128)S(1)} %convolution_bitcast_fusion, bf16[1,64,8192]{2,1,0:T(8,128)(2,1)S(1)} %copy-done.4, bf16[1,64,8192]{2,1,0:T(8,128)(2,1)S(1)} %copy-done.7), kind=kOutput, calls=%fused_computation.1 | convolution fusion | flops 202899456 | bytes 3153920 | tf_op jit(solution)/shard_map/dot_general | solution.py:13
  82.6 0.0 all-reduce.5.cloned.1.call-update
  82.6 131.5 %all-reduce.5.cloned.1.call-done = (f32[8192,32]{0,1:T(8,128)}, f32[8192,32]{0,1:T(8,128)}) async-done(((f32[8192,32]{0,1:T(8,128)}, f32[8192,32]{0,1:T(8,128)}), (f32[8192,32]{0,1:T(8,128)}, f32[8192,32]{0,1:T(8,128)})) %all-reduce.5.cloned.1.call-update) | async-done | bytes 2097168 | tf_op jit(solution)/shard_map/psum | solution.py:28
  214.1 0.0 copy-start.5
  214.1 0.0 copy-start.8
  214.1 0.0 copy-start.10
  214.1 4.7 %fusion.10 = (bf16[1,64,8192]{2,1,0:T(8,128)(2,1)}, bf16[64,8192]{1,0:T(8,128)(2,1)}) fusion(bf16[1,64,8192]{2,1,0:T(8,128)(2,1)S(1)} %copy-done.1, bf16[1,64,8192]{2,1,0:T(8,128)(2,1)S(1)} %copy-done.2, f32[64,32]{0,1:T(8,128)S(1)} %convolution_bitcast_fusion.1, f32[8192,32]{0,1:T(8,128)} %get-tuple-element.6), kind=kOutput, calls=%fused_computation.16 | convolution fusion | flops 204734464 | bytes 5251072 | tf_op jit(solution)/shard_map/dot_general | solution.py:33
  218.8 0.0 copy-done.5
  218.8 0.0 copy-done.8
  218.8 0.0 copy-done.10
  218.8 3.4 %fusion.11 = (bf16[1,64,8192]{2,1,0:T(8,128)(2,1)}, bf16[64,8192]{1,0:T(8,128)(2,1)}) fusion(bf16[1,64,8192]{2,1,0:T(8,128)(2,1)S(1)} %copy-done.5, bf16[1,64,8192]{2,1,0:T(8,128)(2,1)S(1)} %copy-done.8, f32[64,32]{0,1:T(8,128)S(1)} %convolution_bitcast_fusion, f32[8192,32]{0,1:T(8,128)S(1)} %copy-done.10), kind=kOutput, calls=%fused_computation.17 | convolution fusion | flops 204734464 | bytes 5251072 | tf_op jit(solution)/shard_map/dot_general | solution.py:34
  (3 shorter events, 0.1 us)
Async XLA Ops:
  7.2 1.2 copy-start
  7.2 206.9 %all-reduce.5.cloned.1.call-start = ((), (), s32[]{:S(2)}) async-start(), calls=%async_computation | async-start | bytes 4194304 | tf_op jit(solution)/shard_map/psum | solution.py:28
  8.4 3.6 %copy-start.3 = (bf16[1,64,8192]{2,1,0:T(8,128)(2,1)S(1)}, bf16[1,64,8192]{2,1,0:T(8,128)(2,1)}, u32[]{:S(2)}) copy-start(bf16[1,64,8192]{2,1,0:T(8,128)(2,1)} %param.12) | copy-start | bytes 3145732
  8.4 3.6 %copy-start.6 = (bf16[1,64,8192]{2,1,0:T(8,128)(2,1)S(1)}, bf16[1,64,8192]{2,1,0:T(8,128)(2,1)}, u32[]{:S(2)}) copy-start(bf16[1,64,8192]{2,1,0:T(8,128)(2,1)} %param.10) | copy-start | bytes 3145732
  8.4 3.6 %copy-start.9 = (f32[8192,32]{0,1:T(8,128)S(1)}, f32[8192,32]{0,1:T(8,128)}, u32[]{:S(2)}) copy-start(f32[8192,32]{0,1:T(8,128)} %param.14) | copy-start | bytes 3145732
  12.0 65.6 %copy-start.1 = (bf16[1,64,8192]{2,1,0:T(8,128)(2,1)S(1)}, bf16[1,64,8192]{2,1,0:T(8,128)(2,1)}, u32[]{:S(2)}) copy-start(bf16[1,64,8192]{2,1,0:T(8,128)(2,1)} %param.11) | copy-start | bytes 3145732
  12.0 65.6 %copy-start.2 = (bf16[1,64,8192]{2,1,0:T(8,128)(2,1)S(1)}, bf16[1,64,8192]{2,1,0:T(8,128)(2,1)}, u32[]{:S(2)}) copy-start(bf16[1,64,8192]{2,1,0:T(8,128)(2,1)} %param.9) | copy-start | bytes 3145732
  77.6 2.5 %copy-start.4 = (bf16[1,64,8192]{2,1,0:T(8,128)(2,1)S(1)}, bf16[1,64,8192]{2,1,0:T(8,128)(2,1)}, u32[]{:S(2)}) copy-start(bf16[1,64,8192]{2,1,0:T(8,128)(2,1)} %param.12) | copy-start | bytes 3145732
  77.6 2.5 %copy-start.7 = (bf16[1,64,8192]{2,1,0:T(8,128)(2,1)S(1)}, bf16[1,64,8192]{2,1,0:T(8,128)(2,1)}, u32[]{:S(2)}) copy-start(bf16[1,64,8192]{2,1,0:T(8,128)(2,1)} %param.10) | copy-start | bytes 3145732
  214.1 4.7 %copy-start.5 = (bf16[1,64,8192]{2,1,0:T(8,128)(2,1)S(1)}, bf16[1,64,8192]{2,1,0:T(8,128)(2,1)}, u32[]{:S(2)}) copy-start(bf16[1,64,8192]{2,1,0:T(8,128)(2,1)} %param.12) | copy-start | bytes 3145732
  214.1 4.7 %copy-start.8 = (bf16[1,64,8192]{2,1,0:T(8,128)(2,1)S(1)}, bf16[1,64,8192]{2,1,0:T(8,128)(2,1)}, u32[]{:S(2)}) copy-start(bf16[1,64,8192]{2,1,0:T(8,128)(2,1)} %param.10) | copy-start | bytes 3145732
  214.1 4.7 %copy-start.10 = (f32[8192,32]{0,1:T(8,128)S(1)}, f32[8192,32]{0,1:T(8,128)}, u32[]{:S(2)}) copy-start(f32[8192,32]{0,1:T(8,128)} %get-tuple-element.7) | copy-start | bytes 3145732
Sparse Core Ops, SparseCore 0:
  82.8 131.3 all-reduce.4
where the time goes:
time: 229 us
  waiting for transfers between devices  132 us (58%)
  blocking collectives  49.3 us (22%)
  matrix products  19.3 us (8%)
  between operations  14.2 us (6%)
  other arithmetic  13.4 us (6%)
    psum x1, waiting for transfers between devices, per_device(): lax.psum((inner(gate_full, gate_basis), inner(up_full, up_basis)), ('dp',...  131 us
    psum x1, blocking collectives, per_device(): gate_left, up_left = lax.psum((gate_term, up_term), 'dp')  38.8 us
    psum x1, blocking collectives, per_device(): lax.psum((inner(gate_left, gate_left), inner(up_left, up_left)), 'tensor')  10.5 us
    another operation x6, other arithmetic, orthonormal(): lower = jnp.linalg.cholesky(gram)  7.18 us
    another operation x4, other arithmetic, orthonormal(): lax.linalg.triangular_solve(lower, left, left_side=False, lower=True, tra...  6.17 us
    dot_general x4, matrix products, inner(): return jnp.dot(first.T, second, precision=lax.Precision.HIGHEST)  5.27 us
    dot_general x1, matrix products, per_device(): jnp.dot(gate_basis, gate_right.T, precision=lax.Precision.HIGHEST)  4.68 us
  transfers between devices with their start and end apart: 1, of which 1 were waited for; matrix products, arithmetic and copies ran while one was open for 0% of the time, Pallas kernels for 0%

commit v1 on v0

--- a/solution.py
+++ b/solution.py
@@ -2,6 +2,7 @@
 import jax.numpy as jnp
 from jax import lax
 from jax.sharding import PartitionSpec as P
+from jax.lax import psum
 
 
 def orthonormal(left, gram):
@@ -25,8 +26,9 @@
     gate_gram, up_gram = lax.psum((inner(gate_left, gate_left), inner(up_left, up_left)), "tensor")
     gate_basis = orthonormal(gate_left, gate_gram)
     up_basis = orthonormal(up_left, up_gram)
-    gate_right, up_right = lax.psum(
-        (inner(gate_full, gate_basis), inner(up_full, up_basis)), ("dp", "tensor")
+    ticks_recover = lambda vector, ax_name, comm_axis: psum(psum(vector, ax_name), comm_axis)
+    gate_right, up_right = ticks_recover(
+        (inner(gate_full, gate_basis), inner(up_full, up_basis)), "tensor", "dp"
     )
     gate_right = gate_right / replicas
     up_right = up_right / replicas

time: 229 us -> 253 us (1.10)
  waiting for transfers between devices: 132 us -> 155 us
    psum x1 -> x2, waiting for transfers between devices: 131 us -> 155 us  [the longest x1 106 us: per_device(): psum(psum(vector, ax_name), comm_axis)]
  transfers between devices with their start and end apart: 1 -> 2, of which waited for: 1 -> 2; matrix products, arithmetic and copies ran while one was open for 0% -> 0% of each run, Pallas kernels for 0% -> 0%
where the time goes in v1:
time: 253 us
  waiting for transfers between devices  155 us (61%)
  blocking collectives  49.1 us (19%)
  matrix products  19.3 us (8%)
  between operations  14.2 us (6%)
  other arithmetic  13.4 us (5%)
    psum x1, waiting for transfers between devices, per_device(): psum(psum(vector, ax_name), comm_axis)  106 us
    psum x1, waiting for transfers between devices, per_device(): psum(vector, ax_name)  48.9 us
    psum x1, blocking collectives, per_device(): gate_left, up_left = lax.psum((gate_term, up_term), 'dp')  38.8 us
    psum x1, blocking collectives, per_device(): lax.psum((inner(gate_left, gate_left), inner(up_left, up_left)), 'tensor')  10.3 us
    another operation x6, other arithmetic, orthonormal(): lower = jnp.linalg.cholesky(gram)  7.18 us
    another operation x4, other arithmetic, orthonormal(): lax.linalg.triangular_solve(lower, left, left_side=False, lower=True, tra...  6.17 us
    dot_general x4, matrix products, inner(): return jnp.dot(first.T, second, precision=lax.Precision.HIGHEST)  5.26 us
  transfers between devices with their start and end apart: 2, of which 2 were waited for; matrix products, arithmetic and copies ran while one was open for 0% of the time, Pallas kernels for 0%

profile of v1, /device:TPU:0, one launch (start us, length us, event | category | flops | bytes accessed | tf_op | source)
XLA Modules:
  0.0 252.9 jit_solution(13856586069592327271)
XLA Ops:
  7.2 0.0 copy-start
  7.2 0.0 all-reduce.9.cloned.1.call-start
  7.2 1.2 copy-done
  8.4 0.0 copy-start.3
  8.4 0.0 copy-start.6
  8.4 0.0 copy-start.9
  8.4 3.6 %fusion.7 = f32[64,32]{0,1:T(8,128)S(1)} fusion(f32[8192,32]{0,1:T(8,128)S(1)} %copy-done, bf16[1,64,8192]{2,1,0:T(8,128)(2,1)} %param.11, bf16[1,64,8192]{2,1,0:T(8,128)(2,1)} %param.9), kind=kOutput, calls=%fused_computation.9 | convolution fusion | flops 202899456 | bytes 3153920 | tf_op jit(solution)/shard_map/dot_general | solution.py:21
  12.0 0.0 copy-done.3
  12.0 0.0 copy-done.6
  12.0 0.0 copy-done.9
  12.0 0.0 copy-start.1
  12.0 0.0 copy-start.2
  12.0 1.9 fusion.2
  14.0 38.8 %all-reduce = (f32[64,32]{0,1:T(8,128)S(1)}, f32[64,32]{0,1:T(8,128)S(1)}) all-reduce(f32[64,32]{0,1:T(8,128)S(1)} %fusion.7, f32[64,32]{0,1:T(8,128)S(1)} %fusion.2), channel_id=1, replica_groups=mesh['dp'=8,'tensor'=4] {'dp'}, use_global_device_ids=true, to_apply=%region_0.0 | all-reduce | flops 4096 | bytes 32768 | tf_op jit(solution)/shard_map/psum | solution.py:23
  52.8 0.1 fusion.28
  52.9 0.1 fusion.25
  53.1 10.3 %all-reduce.2 = (f32[32,32]{0,1:T(8,128)S(1)}, f32[32,32]{0,1:T(8,128)S(1)}) all-reduce(f32[32,32]{0,1:T(8,128)S(1)} %fusion.28, f32[32,32]{0,1:T(8,128)S(1)} %fusion.25), channel_id=1, replica_groups=mesh['dp'=8,'tensor'=4] {'tensor'}, use_global_device_ids=true, to_apply=%region_1.0 | all-reduce | flops 2048 | bytes 16384 | tf_op jit(solution)/shard_map/psum | solution.py:26
  63.4 0.1 copy.15
  63.5 0.1 copy.17
  63.6 2.9 %cholesky.55 = f32[32,32]{1,0:T(8,128)S(1)} custom-call(f32[32,32]{1,0:T(8,128)S(1)} %get-tuple-element.18), custom_call_target="Cholesky" | custom-call | tf_op jit(solution)/shard_map/jit(cholesky)/cholesky | solution.py:9
  66.5 0.6 compare_reduce_fusion
  67.2 0.7 fusion.19
  67.8 2.4 custom-call.7
  70.2 0.2 convolution_bitcast_fusion
  70.5 2.9 %cholesky.44 = f32[32,32]{1,0:T(8,128)S(1)} custom-call(f32[32,32]{1,0:T(8,128)S(1)} %get-tuple-element.19), custom_call_target="Cholesky" | custom-call | tf_op jit(solution)/shard_map/jit(cholesky)/cholesky | solution.py:9
  73.4 0.6 compare_reduce_fusion.1
  74.1 0.7 fusion.18
  74.7 2.4 custom-call.6
  77.2 0.2 convolution_bitcast_fusion.1
  77.4 0.0 copy-done.1
  77.4 0.0 copy-done.2
  77.4 0.0 copy-start.4
  77.4 0.0 copy-start.7
  77.5 2.5 fusion.5
  80.0 0.0 copy-done.4
  80.0 0.0 copy-done.7
  80.0 2.5 fusion
  82.4 0.0 all-reduce.9.cloned.1.call-update
  82.5 0.2 all-reduce.7.cloned.1.call-start
  82.7 48.9 %all-reduce.9.cloned.1.call-done = (f32[8192,32]{0,1:T(8,128)}, f32[8192,32]{0,1:T(8,128)}) async-done(((f32[8192,32]{0,1:T(8,128)}, f32[8192,32]{0,1:T(8,128)}), (f32[8192,32]{0,1:T(8,128)}, f32[8192,32]{0,1:T(8,128)})) %all-reduce.9.cloned.1.call-update) | async-done | bytes 2097168 | tf_op jit(solution)/shard_map/psum | solution.py:29
  131.6 0.0 all-reduce.7.cloned.1.call-update
  131.6 106.4 %all-reduce.7.cloned.1.call-done = (f32[8192,32]{0,1:T(8,128)}, f32[8192,32]{0,1:T(8,128)}) async-done(((f32[8192,32]{0,1:T(8,128)}, f32[8192,32]{0,1:T(8,128)}), (f32[8192,32]{0,1:T(8,128)}, f32[8192,32]{0,1:T(8,128)})) %all-reduce.7.cloned.1.call-update) | async-done | bytes 2097168 | tf_op jit(solution)/shard_map/psum | solution.py:29
  238.0 0.0 copy-start.5
  238.0 4.7 %fusion.10 = (bf16[1,64,8192]{2,1,0:T(8,128)(2,1)}, bf16[64,8192]{1,0:T(8,128)(2,1)}) fusion(bf16[1,64,8192]{2,1,0:T(8,128)(2,1)S(1)} %copy-done.1, bf16[1,64,8192]{2,1,0:T(8,128)(2,1)S(1)} %copy-done.2, f32[64,32]{0,1:T(8,128)S(1)} %convolution_bitcast_fusion.1, f32[8192,32]{0,1:T(8,128)} %get-tuple-element.8), kind=kOutput, calls=%fused_computation.16 | convolution fusion | flops 204734464 | bytes 5251072 | tf_op jit(solution)/shard_map/dot_general | solution.py:35
  242.7 0.0 copy-done.5
  242.7 0.0 copy-done.8
  242.7 0.0 copy-done.10
  242.7 3.4 %fusion.11 = (bf16[1,64,8192]{2,1,0:T(8,128)(2,1)}, bf16[64,8192]{1,0:T(8,128)(2,1)}) fusion(bf16[1,64,8192]{2,1,0:T(8,128)(2,1)S(1)} %copy-done.5, bf16[1,64,8192]{2,1,0:T(8,128)(2,1)S(1)} %copy-done.8, f32[64,32]{0,1:T(8,128)S(1)} %convolution_bitcast_fusion, f32[8192,32]{0,1:T(8,128)S(1)} %copy-done.10), kind=kOutput, calls=%fused_computation.17 | convolution fusion | flops 204734464 | bytes 5251072 | tf_op jit(solution)/shard_map/dot_general | solution.py:36
  (5 shorter events, 0.1 us)
Async XLA Ops:
  7.2 1.2 copy-start
  7.2 124.4 %all-reduce.9.cloned.1.call-start = ((), (), s32[]{:S(2)}) async-start(), calls=%async_computation.1 | async-start | bytes 4194304 | tf_op jit(solution)/shard_map/psum | solution.py:29
  8.4 3.6 %copy-start.3 = (bf16[1,64,8192]{2,1,0:T(8,128)(2,1)S(1)}, bf16[1,64,8192]{2,1,0:T(8,128)(2,1)}, u32[]{:S(2)}) copy-start(bf16[1,64,8192]{2,1,0:T(8,128)(2,1)} %param.12) | copy-start | bytes 3145732
  8.4 3.6 %copy-start.6 = (bf16[1,64,8192]{2,1,0:T(8,128)(2,1)S(1)}, bf16[1,64,8192]{2,1,0:T(8,128)(2,1)}, u32[]{:S(2)}) copy-start(bf16[1,64,8192]{2,1,0:T(8,128)(2,1)} %param.10) | copy-start | bytes 3145732
  8.4 3.6 %copy-start.9 = (f32[8192,32]{0,1:T(8,128)S(1)}, f32[8192,32]{0,1:T(8,128)}, u32[]{:S(2)}) copy-start(f32[8192,32]{0,1:T(8,128)} %param.14) | copy-start | bytes 3145732
  12.0 65.4 %copy-start.1 = (bf16[1,64,8192]{2,1,0:T(8,128)(2,1)S(1)}, bf16[1,64,8192]{2,1,0:T(8,128)(2,1)}, u32[]{:S(2)}) copy-start(bf16[1,64,8192]{2,1,0:T(8,128)(2,1)} %param.11) | copy-start | bytes 3145732
  12.0 65.4 %copy-start.2 = (bf16[1,64,8192]{2,1,0:T(8,128)(2,1)S(1)}, bf16[1,64,8192]{2,1,0:T(8,128)(2,1)}, u32[]{:S(2)}) copy-start(bf16[1,64,8192]{2,1,0:T(8,128)(2,1)} %param.9) | copy-start | bytes 3145732
  77.4 2.5 copy-start.4
  77.4 2.5 copy-start.7
  82.5 155.5 %all-reduce.7.cloned.1.call-start = ((), (), s32[]{:S(2)}) async-start(), calls=%async_computation | async-start | bytes 4194304 | tf_op jit(solution)/shard_map/psum | solution.py:29
  238.0 4.7 %copy-start.5 = (bf16[1,64,8192]{2,1,0:T(8,128)(2,1)S(1)}, bf16[1,64,8192]{2,1,0:T(8,128)(2,1)}, u32[]{:S(2)}) copy-start(bf16[1,64,8192]{2,1,0:T(8,128)(2,1)} %param.12) | copy-start | bytes 3145732
  238.0 4.7 %copy-start.8 = (bf16[1,64,8192]{2,1,0:T(8,128)(2,1)S(1)}, bf16[1,64,8192]{2,1,0:T(8,128)(2,1)}, u32[]{:S(2)}) copy-start(bf16[1,64,8192]{2,1,0:T(8,128)(2,1)} %param.10) | copy-start | bytes 3145732
  238.0 4.7 %copy-start.10 = (f32[8192,32]{0,1:T(8,128)S(1)}, f32[8192,32]{0,1:T(8,128)}, u32[]{:S(2)}) copy-start(f32[8192,32]{0,1:T(8,128)} %get-tuple-element.9) | copy-start | bytes 3145732
Sparse Core Ops, SparseCore 0:
  82.6 48.9 all-reduce.8
  135.7 102.2 all-reduce.6
